TPU v7x, 1024 devices: a whole 4x4x32 slice. The times are simulated.
1024 devices in a mesh: dp: 8 (over y, core), ctx: 4 (over x), expert: 32 (over z).
Axes of the slice: x: 4, y: 4, z: 32, core: 2. Of those that a mesh axis runs over, the one named last changes fastest.
Arguments:
- out_grad: bfloat16 [8192, 7168], P(('ctx', 'expert'), 'dp'), may hold values from -6 to 6
- expert_ids: int32 [8192, 8], P(('ctx', 'expert')), may hold values from 0 to 31, all different within a row; in each aligned block of 64 rows (0 to 63, 64 to 127, ...) at most 32 rows name the same one
- gates: bfloat16 [8192, 8], P(('ctx', 'expert')), may hold values from 0.049804688 to 1
- hidden_saved: bfloat16 [131072, 1024], P(('ctx', 'expert')), may hold values from -0.1796875 to 0.1796875
- w_down: bfloat16 [32, 1024, 7168], P('expert', None, 'dp'), may hold values from -0.0625 to 0.0625
Outputs:
- d_hidden: bfloat16 [131072, 1024], P(('ctx', 'expert'), 'dp')
- w_grad: float32 [32, 1024, 7168], P('expert', 'ctx', 'dp')
- gate_grad: float32 [8192, 8], P(('ctx', 'expert'))
Inputs may be any that keep to these rules, and one draw needn't show every extreme that they name: `expert_ids`: each token names 8 different experts. Among the 64 x 8 choices of one device's tokens, no expert is named more than 32 times, a bound that some block reaches.
All inputs are finite; a program needn't handle non-finite values.
Results may differ from a plain program's by a relative error of at most 0.019.
Values may be sent and summed in bfloat16 or wider, within the bound.
A program may use at most 32 MiB of HBM per device.

v0:
```python
import jax
import jax.numpy as jnp
from jax import lax
from jax.sharding import PartitionSpec as P

TOP = 8


def gate_sum(gate_piece):
    return lax.psum(gate_piece, "dp")


def body(out_grad, expert_ids, gates, hidden_saved, w_down):
    tok_count, width_part = out_grad.shape
    peer_count = lax.axis_size("expert")
    local_count = w_down.shape[0]
    expert_count = local_count * peer_count
    ff_all = w_down.shape[1]
    slots = hidden_saved.shape[0] // local_count
    capacity = slots // peer_count
    routed = tok_count * TOP
    choice_ids = expert_ids.reshape(-1)
    onehot = (choice_ids[:, None] == jnp.arange(expert_count, dtype=jnp.int32)[None, :]).astype(
        jnp.int32
    )
    earlier = jnp.cumsum(onehot, axis=0) - onehot
    position = jnp.sum(earlier * onehot, axis=1)
    target = choice_ids * capacity + position
    owner_index = (
        jnp.full((expert_count * capacity,), routed, jnp.int32)
        .at[target]
        .set(jnp.arange(routed, dtype=jnp.int32))
    )
    alive = owner_index < routed
    clipped = jnp.minimum(owner_index, routed - 1)
    send_rows = jnp.where(alive[:, None], out_grad[clipped // TOP], jnp.zeros((), jnp.bfloat16))
    send_rows = send_rows.reshape(expert_count, capacity, width_part)
    send_gates = jnp.where(alive, gates.reshape(-1)[clipped], jnp.zeros((), jnp.bfloat16))
    send_gates = send_gates.reshape(expert_count, capacity)
    recv_rows, recv_gates = (
        lax.all_to_all(send_rows, "expert", split_axis=0, concat_axis=1, tiled=True),
        lax.all_to_all(send_gates, "expert", split_axis=0, concat_axis=1, tiled=True),
    )
    partial_value = jnp.einsum(
        "esd,efd->esf", recv_rows, w_down, preferred_element_type=jnp.float32
    )
    hidden = hidden_saved.reshape(local_count, slots, ff_all)
    gate_wide = recv_gates.astype(jnp.float32)
    lane_count = ff_all // lax.axis_size("dp")
    offset = lax.axis_index("dp") * lane_count
    hidden_share = lax.psum_scatter(
        partial_value.astype(jnp.bfloat16), "dp", scatter_dimension=2, tiled=True
    ).astype(jnp.float32)
    own_hidden = lax.dynamic_slice_in_dim(hidden, offset, lane_count, 2)
    gate_total = gate_sum(jnp.sum(own_hidden.astype(jnp.float32) * hidden_share, axis=2))
    returned = lax.all_to_all(gate_total, "expert", split_axis=1, concat_axis=0, tiled=True)
    gate_grad = returned.reshape(-1)[target].reshape(tok_count, TOP)
    d_hidden = (
        (gate_wide[:, :, None] * hidden_share)
        .astype(jnp.bfloat16)
        .reshape(local_count * slots, lane_count)
    )
    scaled = (gate_wide[:, :, None] * recv_rows.astype(jnp.float32)).astype(jnp.bfloat16)
    weight_share = lax.psum_scatter(
        jnp.einsum("esf,esd->fed", hidden, scaled, preferred_element_type=jnp.float32).astype(
            jnp.bfloat16
        ),
        "ctx",
        scatter_dimension=0,
        tiled=True,
    ).astype(jnp.float32)
    w_grad = jnp.transpose(weight_share, (1, 0, 2))
    return (d_hidden, w_grad, gate_grad)


def solution(mesh):
    return jax.shard_map(
        body,
        mesh=mesh,
        in_specs=(
            P(("ctx", "expert"), "dp"),
            P(("ctx", "expert"), None),
            P(("ctx", "expert"), None),
            P(("ctx", "expert"), None),
            P("expert", None, "dp"),
        ),
        out_specs=(
            P(("ctx", "expert"), "dp"),
            P("expert", "ctx", "dp"),
            P(("ctx", "expert"), None),
        ),
        check_vma=False,
    )
```

profile of v0, /device:TPU:1, one launch (start us, length us, event | category | flops | bytes accessed | tf_op | source)
XLA Modules:
  0.0 367.5 jit_solution(3224822992683478476)
XLA Ops:
  7.2 0.0 copy-start
  7.2 0.0 copy-start.1
  7.2 0.0 reduce-scatter.7.cloned.1.call-start
  7.2 0.8 broadcast_multiply_fusion
  8.1 0.8 copy.17
  8.8 0.1 eq.29
  8.9 0.1 eq.25
  9.0 0.8 copy.20
  9.8 0.1 reshape.149
  9.9 0.1 copy.16
  10.0 0.1 mul.50
  10.1 1.2 reduce-window.6
  11.3 0.2 slice_reduce_fusion
  11.5 0.1 fusion.8
  11.7 2.4 scatter_custom_fusion
  14.1 6.8 %gather_fusion = bf16[1024]{0:T(1024)(128)(2,1)S(1)} fusion(bf16[512]{0:T(512)(128)(2,1)S(1)} %reshape.149, s32[1024]{0:T(1024)S(1)} %get-tuple-element.16), kind=kCustom, calls=%fused_computation | custom fusion | bytes 8192 | tf_op jit(solution)/shard_map/gather | solution.py:38
  20.9 0.1 broadcast_in_dim.32
  21.0 0.0 copy-done.1
  21.0 5.3 %gather_fusion.1 = bf16[1024,896]{1,0:T(8,128)(2,1)} fusion(bf16[64,896]{1,0:T(8,128)(2,1)S(1)} %copy-done.1, s32[1024]{0:T(1024)S(1)} %get-tuple-element.17), kind=kCustom, calls=%fused_computation.1 | custom fusion | bytes 3674112 | tf_op jit(solution)/shard_map/gather | solution.py:36
  26.3 1.8 broadcast_select_fusion
  28.1 204.7 %all_to_all.36 = bf16[32,32,896]{2,1,0:T(8,128)(2,1)S(1)} all-to-all(bf16[32,32,896]{2,1,0:T(8,128)(2,1)S(1)} %broadcast_select_fusion), channel_id=1, replica_groups=mesh['dp'=8,'ctx'=4,'expert'=32] {'expert'}, dimensions={0} | all-to-all | bytes 3670016 | tf_op jit(solution)/shard_map/all_to_all | solution.py:41
  232.8 0.0 copy-start.2
  232.8 1.2 copy-done.2
  234.1 0.0 copy-done
  234.1 3.7 %convert_bitcast_fusion = bf16[1,1024,1024]{2,1,0:T(8,128)(2,1)} fusion(bf16[1024,896]{1,0:T(8,128)(2,1)S(1)} %bitcast.53, bf16[1,1024,896]{2,1,0:T(8,128)(2,1)S(1)} %copy-done), kind=kOutput, calls=%fused_computation.6 | convolution fusion | flops 1880096768 | bytes 5767168 | tf_op jit(solution)/shard_map/esd,efd->esf/dot_general | solution.py:44
  237.8 10.8 %copy.24 = bf16[1,1024,1024]{1,0,2:T(2,128)(2,1)} copy(bf16[1,1024,1024]{2,1,0:T(8,128)(2,1)} %convert_bitcast_fusion) | data formatting | bytes 4194304
  248.6 4.3 %copy.30 = bf16[1024,1,1024]{2,0,1:T(8,128)(2,1)} copy(bf16[1024,1,1024]{2,1,0:T(2,128)(2,1)} %bitcast.50) | data formatting | bytes 4194304
  252.9 0.0 reduce-scatter.7.cloned.1.call-update
  252.9 0.0 reduce-scatter.5.cloned.1.call-start
  253.0 0.1 all_to_all.32
  253.1 25.5 %all_to_all.37 = bf16[32,1,32]{2,1,0:T(2,128)(2,1)S(1)} all-to-all(bf16[32,1,32]{2,1,0:T(2,128)(2,1)S(1)} %all_to_all.32), channel_id=1, replica_groups=mesh['dp'=8,'ctx'=4,'expert'=32] {'expert'}, dimensions={0} | all-to-all | bytes 4096 | tf_op jit(solution)/shard_map/all_to_all | solution.py:42
  278.5 0.1 convert_reduce_fusion
  278.6 0.1 reshape.156
  278.7 5.6 %convert_bitcast_fusion.1 = bf16[1024,1,896]{0,2,1:T(8,128)(2,1)} fusion(bf16[1024,1024]{1,0:T(8,128)(2,1)} %param.8, bf16[1024,896]{1,0:T(8,128)(2,1)} %bitcast.54, f32[1024]{0:T(1024)S(1)} %reshape.156), kind=kOutput, calls=%fused_computation.9 | convolution fusion | flops 1882718208 | bytes 5771264 | tf_op jit(solution)/shard_map/esf,esd->fed/dot_general | solution.py:65
  284.3 0.0 reduce-scatter.5.cloned.1.call-update
  284.3 3.5 reduce-scatter.7.cloned.1.call-done
  287.8 1.2 reshape_bitcast_fusion
  289.1 0.4 copy.25
  289.5 1.9 fusion.4
  291.4 0.1 all_to_all.30
  291.5 23.8 %psum.7 = f32[1,32,32]{2,0,1:T(1,128)} all-reduce(f32[1,32,32]{2,0,1:T(1,128)S(1)} %all_to_all.30), channel_id=1, replica_groups=mesh['dp'=8,'ctx'=4,'expert'=32] {'dp'}, use_global_device_ids=true, to_apply=%region_7.8 | all-reduce | flops 1024 | bytes 8192 | tf_op jit(solution)/shard_map/psum | solution.py:10
  315.2 19.9 %all-to-all-start.2 = ((f32[1,32,32]{2,0,1:T(1,128)}), f32[1,32,32]{2,0,1:T(1,128)S(1)}, u32[]{:S(2)}, u32[]{:S(2)}) async-start(f32[1,32,32]{2,0,1:T(1,128)} %psum.7), calls=%async_computation.3 | async-start | bytes 32768 | tf_op jit(solution)/shard_map/all_to_all | solution.py:56
  335.2 0.0 reduce-scatter.5.cloned.1.call-done
  335.2 1.1 bitcast_convert_fusion
  336.3 1.2 copy.22
  337.5 18.8 %all-to-all-done.2 = f32[1,32,32]{2,0,1:T(1,128)S(1)} async-done(((f32[1,32,32]{2,0,1:T(1,128)}), f32[1,32,32]{2,0,1:T(1,128)S(1)}, u32[]{:S(2)}, u32[]{:S(2)}) %all-to-all-start.2) | async-done | bytes 4128 | tf_op jit(solution)/shard_map/all_to_all | solution.py:56
  356.3 0.5 broadcast.103
  356.8 0.7 reduce.10
  357.5 0.1 reshape.153
  357.6 2.3 gather_fusion.2
  359.9 0.1 reshape.154
  360.0 0.7 copy.23
  (8 shorter events, 0.1 us)
Async XLA Ops:
  7.2 226.9 %copy-start = (bf16[1,1024,896]{2,1,0:T(8,128)(2,1)S(1)}, bf16[1,1024,896]{2,1,0:T(8,128)(2,1)}, u32[]{:S(2)}) copy-start(bf16[1,1024,896]{2,1,0:T(8,128)(2,1)} %param.9) | copy-start | bytes 5505028
  7.2 13.9 %copy-start.1 = (bf16[64,896]{1,0:T(8,128)(2,1)S(1)}, bf16[64,896]{1,0:T(8,128)(2,1)}, u32[]{:S(2)}) copy-start(bf16[64,896]{1,0:T(8,128)(2,1)} %param.5) | copy-start | bytes 344068
  7.2 280.6 %reduce-scatter.7.cloned.1.call-start = ((), (), s32[]{:S(2)}) async-start(), calls=%async_computation.6 | async-start | bytes 2359296
  232.8 1.2 copy-start.2
  252.9 82.3 %reduce-scatter.5.cloned.1.call-start = ((), (), s32[]{:S(2)}) async-start(), calls=%async_computation.5 | async-start | bytes 2293760 | tf_op jit(solution)/shard_map/reduce_scatter | solution.py:64
  315.2 41.1 %all-to-all-start.2 = ((f32[1,32,32]{2,0,1:T(1,128)}), f32[1,32,32]{2,0,1:T(1,128)S(1)}, u32[]{:S(2)}, u32[]{:S(2)}) async-start(f32[1,32,32]{2,0,1:T(1,128)} %psum.7), calls=%async_computation.3 | async-start | bytes 32768 | tf_op jit(solution)/shard_map/all_to_all | solution.py:56
Sparse Core Ops, SparseCore 0:
  253.1 34.7 reduce-scatter.6
  291.3 43.7 reduce-scatter.4
where the time goes:
time: 372 us; the launch traced here: 367 us
  blocking collectives  254 us (68%)
  local copies, waits for them, and re-layouts  40 us (11%)
  waiting for transfers between devices  22.3 us (6%)
  starting transfers between devices  20 us (5%)
  between operations  14.2 us (4%)
  matrix products  9.32 us (3%)
  other arithmetic  7.65 us (2%)
    all_to_all x1, blocking collectives, body(): lax.all_to_all(send_rows, 'expert', split_axis=0, concat_axis=1, tiled=True)  205 us
    all_to_all x1, blocking collectives, body(): lax.all_to_all(send_gates, 'expert', split_axis=0, concat_axis=1, tiled=T...  25.5 us
    psum x1, blocking collectives, gate_sum(): return lax.psum(gate_piece, 'dp')  23.8 us
    unnamed x14, local copies, waits for them, and re-layouts  21.5 us
    all_to_all x1, starting transfers between devices, body(): lax.all_to_all(gate_total, 'expert', split_axis=1, concat_axis=0, tiled=T...  19.9 us
    all_to_all x1, waiting for transfers between devices, body(): lax.all_to_all(gate_total, 'expert', split_axis=1, concat_axis=0, tiled=T...  18.8 us
  transfers between devices with their start and end apart: 3, of which 2 were waited for; matrix products, arithmetic and copies ran while one was open for 3% of the time, Pallas kernels for 0%

commit v1 on v0

v1 whole, which is shorter than its diff:
```python
import functools

import jax
import jax.numpy as jnp
from jax import lax
from jax.experimental import pallas as pl
from jax.experimental.pallas import tpu as pltpu
from jax.sharding import PartitionSpec as P

MESH = pl.DeviceIdType.MESH
BF = jnp.bfloat16
F32 = jnp.float32

NZ = 32
NC = 4
ND = 8
TOK = 64
CAP = 32
FF = 1024
WID = 896
TILES = WID // 128
SH = FF // ND
FQ = FF // NC
META = 16
ROWS = META + TOK * TILES
GB = 8
NG = NZ // GB
GR = GB * CAP
GT = GB * TOK
CHUNKS = ((0, META + 2 * TOK), (META + 2 * TOK, 2 * TOK), (META + 4 * TOK, 2 * TOK), (META + 6 * TOK, TOK))
NCH = len(CHUNKS)


def kernel(
    x_ref, ids_ref, gates_ref, hid_hbm, w_hbm,
    dh_ref, wg_ref, gg_ref,
    gat, hid, wv, acc, rows_s, scaled_s, pown, sel_s, gcol_s,
    pbuf, prec, qbuf, qrec, gsend, gback, part_s, parts,
    xa, xb1, xb2, ra, rb1, rb2,
    load_sem, zs, zr, cs, cr, ys, yr, gs, gr, ps, pr, xs, xr,
):
    z = lax.axis_index("expert")
    dp = lax.axis_index("dp")
    cx = lax.axis_index("ctx")
    core = lax.rem(dp, 2)
    yy = dp // 2
    zright = lax.rem(z + 1, NZ)
    zleft = lax.rem(z + NZ - 1, NZ)
    cright = lax.rem(cx + 1, NC)
    cleft = lax.rem(cx + NC - 1, NC)
    copp = lax.rem(cx + 2, NC)
    partner = dp + 1 - 2 * core

    barrier = pltpu.get_barrier_semaphore()
    for nb in (zright, zleft):
        pl.semaphore_signal(barrier, inc=1, device_id={"expert": nb}, device_id_type=MESH)
    for nb in (cright, cleft):
        pl.semaphore_signal(barrier, inc=1, device_id={"ctx": nb}, device_id_type=MESH)
    for i in range(1, ND):
        pl.semaphore_signal(
            barrier, inc=1, device_id={"dp": lax.rem(dp + i, ND)}, device_id_type=MESH
        )

    loads = (
        pltpu.make_async_copy(hid_hbm, hid, load_sem.at[0]),
        pltpu.make_async_copy(w_hbm.at[:, core], wv.at[0], load_sem.at[1]),
        pltpu.make_async_copy(w_hbm.at[:, 1 - core], wv.at[1], load_sem.at[2]),
    )
    for load in loads:
        load.start()

    e_iota = lax.broadcasted_iota(jnp.int32, (NZ, TOK), 0)
    gate_tab = jnp.zeros((NZ, TOK), F32)
    gates = gates_ref[...].astype(F32)
    for k in range(8):
        gate_tab = gate_tab + jnp.where(e_iota == ids_ref[k : k + 1, :], gates[k : k + 1, :], 0.0)
    gat[0, 0:META, :] = jnp.concatenate([gate_tab[0:META], gate_tab[META:]], axis=1).astype(BF)
    for j in range(TILES):
        gat[0, META + j * TOK : META + (j + 1) * TOK, :] = x_ref[:, j * 128 : (j + 1) * 128]

    pl.semaphore_wait(barrier, 4 + ND - 1)

    def hop(d, c, k):
        lo, n = CHUNKS[c]
        if d == 0:
            src, dst, dev = jnp.maximum(2 * k - 1, 0), 2 * k + 1, zright
        else:
            src, dst, dev = 2 * k, 2 * k + 2, zleft
        return pltpu.make_async_remote_copy(
            src_ref=gat.at[src, pl.ds(lo, n)],
            dst_ref=gat.at[dst, pl.ds(lo, n)],
            send_sem=zs.at[d, c, k],
            recv_sem=zr.at[d, c, k],
            device_id={"expert": dev},
            device_id_type=MESH,
        )

    for c in range(NCH):
        for d in range(2):
            hop(d, c, jnp.int32(0)).start()

    for load in loads:
        load.wait()
    acc[...] = jnp.zeros_like(acc)

    def ring_step(k):
        for c in range(NCH):
            hop(0, c, k).wait_recv()

            @pl.when(k < 15)
            def _():
                hop(0, c, k + 1).start()
                hop(1, c, k).wait_recv()

            @pl.when(k < 14)
            def _():
                hop(1, c, k + 1).start()

    def source_of(g, i):
        dist = GB // 2 * g + (i + 1) // 2
        return lax.rem(z + dist if i % 2 == 0 else z - dist + NZ, NZ)

    def rows_of_group(g):
        base = g * GB
        lane = lax.broadcasted_iota(jnp.int32, (GB, 128), 1)
        row = lax.broadcasted_iota(jnp.int32, (GB, 128), 0)
        tab = gat[pl.ds(base, GB), 0:META, :].astype(F32)
        sub = lax.broadcasted_iota(jnp.int32, (GB, META, 128), 1)
        mine = jnp.sum(jnp.where(sub == lax.rem(z, META), tab, 0.0), axis=1)
        odd = lax.rem(row, 2)
        mine = jnp.where(odd == z // META, mine, pltpu.roll(mine, TOK, 1))
        mine = jnp.where(lane // TOK == odd, mine, 0.0)
        named = mine > 0.0
        t0 = lax.broadcasted_iota(jnp.int32, (128, 128), 0)
        t1 = lax.broadcasted_iota(jnp.int32, (128, 128), 1)
        before = jnp.where((t0 < t1) & (t0 // TOK == t1 // TOK), 1.0, 0.0).astype(BF)
        count = jnp.dot(
            jnp.where(named, 1.0, 0.0).astype(BF), before, preferred_element_type=F32
        ).astype(jnp.int32)
        target = jnp.where(named, lax.rem(row, 4) * CAP + count, -1)
        slot = lax.broadcasted_iota(jnp.int32, (128, 128), 0)
        for h in range(2):
            sel, gsel = [], []
            for j in range(2):
                a = 4 * h + 2 * j
                t = jnp.maximum(target[a : a + 1], target[a + 1 : a + 2])
                gv = mine[a : a + 1] + mine[a + 1 : a + 2]
                one = slot == t
                sel.append(jnp.where(one, 1.0, 0.0))
                gsel.append(jnp.where(one, gv, 0.0))
            sel = jnp.concatenate(sel, axis=1)
            gsel = jnp.concatenate(gsel, axis=1)
            sel_s[h] = sel
            gcol_s[h * 128 : (h + 1) * 128, :] = jnp.sum(gsel, axis=1, keepdims=True)
            sel = sel.astype(BF)
            gsel = gsel.astype(BF)
            for j in range(TILES):
                xt = gat[
                    pl.ds(base + 4 * h, 4), META + j * TOK : META + (j + 1) * TOK, :
                ].reshape(4 * TOK, 128)
                cols = slice(j * 128, (j + 1) * 128)
                rows_s[h * 128 : (h + 1) * 128, cols] = jnp.dot(
                    sel, xt, preferred_element_type=F32
                ).astype(BF)
                scaled_s[h * 128 : (h + 1) * 128, cols] = jnp.dot(
                    gsel, xt, preferred_element_type=F32
                ).astype(BF)

    def partial_of(which, y):
        return lax.dot_general(
            rows_s[...], wv[which, y], (((1,), (1,)), ((), ())), preferred_element_type=F32
        )

    def to_partner(g):
        return pltpu.make_async_remote_copy(
            src_ref=pbuf.at[g],
            dst_ref=prec.at[g],
            send_sem=cs.at[g],
            recv_sem=cr.at[g],
            device_id={"dp": partner},
            device_id_type=MESH,
        )

    def to_y(g, i):
        return pltpu.make_async_remote_copy(
            src_ref=qbuf.at[g, i - 1],
            dst_ref=qrec.at[g, i - 1],
            send_sem=ys.at[g, i - 1],
            recv_sem=yr.at[g, i - 1],
            device_id={"dp": lax.rem(dp + 2 * i, ND)},
            device_id_type=MESH,
        )

    def send_partials(g):
        for y in range(4):
            pbuf[g, y] = partial_of(1, y).astype(BF)
        to_partner(g).start()

    def own_partials():
        for y in range(4):
            pown[y] = partial_of(0, y).astype(BF)

    def contribute(g, share):
        parts_h = [
            hid[source_of(g, i), :, pl.ds(pl.multiple_of(share * FQ, FQ), FQ)] for i in range(GB)
        ]
        acc[share] += lax.dot_general(
            jnp.concatenate(parts_h, axis=0),
            scaled_s[...],
            (((0,), (0,)), ((), ())),
            preferred_element_type=F32,
        )

    def sum_cores(g):
        to_partner(g).wait_recv()
        for i in range(1, 4):
            y = lax.rem(yy + i, 4)
            qbuf[g, i - 1] = (pown[y].astype(F32) + prec[g, y].astype(F32)).astype(BF)
            to_y(g, i).start()

    def to_home(p, s):
        return pltpu.make_async_remote_copy(
            src_ref=gsend.at[p // 2],
            dst_ref=gback.at[z],
            send_sem=gs.at[p],
            recv_sem=gr.at[z],
            device_id={"expert": s},
            device_id_type=MESH,
        )

    def finish_rows(g):
        total = pown[yy].astype(F32) + prec[g, yy].astype(F32)
        for i in range(1, 4):
            to_y(g, i).wait_recv()
            total = total + qrec[g, i - 1].astype(F32)
        dh = (gcol_s[...] * total).astype(BF)
        own = []
        for i in range(GB):
            s = source_of(g, i)
            dh_ref[s] = dh[i * CAP : (i + 1) * CAP]
            own.append(hid[s, :, pl.ds(pl.multiple_of(dp * SH, SH), SH)])
        own = jnp.concatenate(own, axis=0).astype(F32)
        col = jnp.sum(own * total, axis=1, keepdims=True)
        for h in range(2):
            back = jnp.sum(sel_s[h] * col[h * 128 : (h + 1) * 128], axis=0, keepdims=True)
            for j in range(2):
                gsend[g * 4 + 2 * h + j] = back[:, j * 128 : (j + 1) * 128]
        for i in range(GB):
            p = g * GB + i
            if i == 0:

                @pl.when(g > 0)
                def _():
                    to_home(p, source_of(g, i)).start()

                @pl.when(g == 0)
                def _():
                    gback[z] = gsend[0]
            else:
                to_home(p, source_of(g, i)).start()

    @pl.loop(0, NG)
    def _(g):
        ring_step(4 * g)

        @pl.when(g > 0)
        def _():
            rows_of_group(g - 1)
            send_partials(g - 1)

        ring_step(4 * g + 1)

        @pl.when(g > 0)
        def _():
            own_partials()
            contribute(g - 1, jnp.int32(0))
            contribute(g - 1, jnp.int32(1))

        ring_step(4 * g + 2)

        @pl.when(g > 0)
        def _():
            contribute(g - 1, jnp.int32(2))
            contribute(g - 1, jnp.int32(3))
            sum_cores(g - 1)

        ring_step(4 * g + 3)

        @pl.when(g > 0)
        def _():
            finish_rows(g - 1)

    half = FQ // 2

    def to_x(kind, d):
        src = (xa, xb1, xb2)[kind]
        dst = (ra, rb1, rb2)[kind]
        return pltpu.make_async_remote_copy(
            src_ref=src.at[d],
            dst_ref=dst.at[d],
            send_sem=xs.at[kind, d],
            recv_sem=xr.at[kind, d],
            device_id={"ctx": (cright, cleft)[d]},
            device_id_type=MESH,
        )

    last = jnp.int32(NG - 1)
    rows_of_group(last)
    contribute(last, copp)
    for d in range(2):
        xa[d] = acc[copp, d * half : (d + 1) * half].astype(BF)
        to_x(0, d).start()
    send_partials(last)
    contribute(last, cright)
    contribute(last, cleft)
    xb1[0] = acc[cright, half:].astype(BF)
    to_x(1, 0).start()
    xb1[1] = acc[cleft, :half].astype(BF)
    to_x(1, 1).start()
    own_partials()
    sum_cores(last)
    to_x(0, 0).wait_recv()
    xb2[0] = (acc[cright, :half] + ra[0].astype(F32)).astype(BF)
    to_x(2, 0).start()
    to_x(0, 1).wait_recv()
    xb2[1] = (acc[cleft, half:] + ra[1].astype(F32)).astype(BF)
    to_x(2, 1).start()
    contribute(last, cx)
    finish_rows(last)

    def from_home(e):
        return pltpu.make_async_remote_copy(
            src_ref=gsend.at[0],
            dst_ref=gback.at[e],
            send_sem=gs.at[0],
            recv_sem=gr.at[e],
            device_id={"expert": e},
            device_id_type=MESH,
        )

    @pl.loop(1, NZ)
    def _(i):
        from_home(lax.rem(z + i, NZ)).wait_recv()

    back = gback[...].reshape(NZ, 128)
    e2 = lax.broadcasted_iota(jnp.int32, (NZ, 128), 0)
    dist = lax.rem(e2 - z + NZ, NZ)
    swap = (dist >= 1) & (dist <= NZ // 2)
    back = jnp.where(swap, pltpu.roll(back, TOK, 1), back)[:, 0:TOK]
    mine = []
    for k in range(8):
        mine.append(
            jnp.sum(jnp.where(e_iota == ids_ref[k : k + 1, :], back, 0.0), axis=0, keepdims=True)
        )
    mine = jnp.concatenate(mine, axis=0)
    part_s[...] = jnp.concatenate([mine, jnp.zeros_like(mine)], axis=1)

    def to_dp(i):
        return pltpu.make_async_remote_copy(
            src_ref=part_s,
            dst_ref=parts.at[i - 1],
            send_sem=ps.at[i - 1],
            recv_sem=pr.at[i - 1],
            device_id={"dp": lax.rem(dp + i, ND)},
            device_id_type=MESH,
        )

    for i in range(1, ND):
        to_dp(i).start()

    to_x(1, 0).wait_recv()
    to_x(1, 1).wait_recv()
    to_x(2, 0).wait_recv()
    wg_ref[:half] = acc[cx, :half] + rb2[0].astype(F32) + rb1[1].astype(F32)
    to_x(2, 1).wait_recv()
    wg_ref[half:] = acc[cx, half:] + rb1[0].astype(F32) + rb2[1].astype(F32)

    for i in range(1, ND):
        to_dp(i).wait_recv()
    total = jnp.zeros((8, 128), F32)
    for j in range(ND):
        i = lax.rem(dp - j + ND, ND)
        total = total + jnp.where(i == 0, part_s[...], parts[jnp.maximum(i - 1, 0)])
    gg_ref[...] = total[:, 0:TOK]

    @pl.loop(0, 16)
    def _(k):
        for c in range(NCH):
            hop(0, c, k).wait_send()

            @pl.when(k < 15)
            def _():
                hop(1, c, k).wait_send()

    @pl.loop(0, NG)
    def _(g):
        to_partner(g).wait_send()
        for i in range(1, 4):
            to_y(g, i).wait_send()

    @pl.loop(1, NZ)
    def _(p):
        to_home(p, zright).wait_send()

    for i in range(1, ND):
        to_dp(i).wait_send()
    for kind in range(3):
        for d in range(2):
            to_x(kind, d).wait_send()


def body(out_grad, expert_ids, gates, hidden_saved, w_down):
    any_spec = pl.BlockSpec(memory_space=pl.ANY)
    vmem = pl.BlockSpec(memory_space=pltpu.VMEM)
    half = FQ // 2
    dma = pltpu.SemaphoreType.DMA
    d_hidden, w_grad, gate_grad = pl.pallas_call(
        kernel,
        out_shape=(
            jax.ShapeDtypeStruct((NZ, CAP, SH), BF),
            jax.ShapeDtypeStruct((FQ, WID), F32),
            jax.ShapeDtypeStruct((8, TOK), F32),
        ),
        in_specs=[vmem, vmem, vmem, any_spec, any_spec],
        out_specs=[vmem, vmem, vmem],
        scratch_shapes=[
            pltpu.VMEM((NZ, ROWS, 128), BF),
            pltpu.VMEM((NZ, CAP, FF), BF),
            pltpu.VMEM((2, 4, SH, WID), BF),
            pltpu.VMEM((NC, FQ, WID), F32),
            pltpu.VMEM((GR, WID), BF),
            pltpu.VMEM((GR, WID), BF),
            pltpu.VMEM((4, GR, SH), BF),
            pltpu.VMEM((2, 128, 256), F32),
            pltpu.VMEM((GR, 1), F32),
            pltpu.VMEM((NG, 4, GR, SH), BF),
            pltpu.VMEM((NG, 4, GR, SH), BF),
            pltpu.VMEM((NG, 3, GR, SH), BF),
            pltpu.VMEM((NG, 3, GR, SH), BF),
            pltpu.VMEM((NZ // 2, 1, 128), F32),
            pltpu.VMEM((NZ, 1, 128), F32),
            pltpu.VMEM((8, 128), F32),
            pltpu.VMEM((ND - 1, 8, 128), F32),
            pltpu.VMEM((2, half, WID), BF),
            pltpu.VMEM((2, half, WID), BF),
            pltpu.VMEM((2, half, WID), BF),
            pltpu.VMEM((2, half, WID), BF),
            pltpu.VMEM((2, half, WID), BF),
            pltpu.VMEM((2, half, WID), BF),
            dma((3,)),
            dma((2, NCH, 16)),
            dma((2, NCH, 16)),
            dma((NG,)),
            dma((NG,)),
            dma((NG, 3)),
            dma((NG, 3)),
            dma((NZ,)),
            dma((NZ,)),
            dma((ND - 1,)),
            dma((ND - 1,)),
            dma((3, 2)),
            dma((3, 2)),
        ],
        compiler_params=pltpu.CompilerParams(
            collective_id=0, has_side_effects=True, vmem_limit_bytes=48 * 2**20
        ),
        cost_estimate=pl.CostEstimate(
            flops=4 * 1024 * 1024 * 896, bytes_accessed=6 * 2**20, transcendentals=0
        ),
    )(
        out_grad,
        expert_ids.T,
        gates.T,
        hidden_saved.reshape(NZ, CAP, FF),
        w_down.reshape(4, 2, SH, WID),
    )
    return (
        d_hidden.reshape(NZ * CAP, SH),
        w_grad.reshape(1, FQ, WID),
        gate_grad.T,
    )


def solution(mesh):
    return jax.shard_map(
        body,
        mesh=mesh,
        in_specs=(
            P(("ctx", "expert"), "dp"),
            P(("ctx", "expert"), None),
            P(("ctx", "expert"), None),
            P(("ctx", "expert"), None),
            P("expert", None, "dp"),
        ),
        out_specs=(
            P(("ctx", "expert"), "dp"),
            P("expert", "ctx", "dp"),
            P(("ctx", "expert"), None),
        ),
        check_vma=False,
    )
```

time: 372 us -> 118 us (0.32); the launches traced: 367 us -> 118 us
  blocking collectives: 254 us -> 0 us
  Pallas kernels: 0 us -> 110 us
  local copies, waits for them, and re-layouts: 40 us -> 7.57 us
  waiting for transfers between devices: 22.3 us -> 0 us
  starting transfers between devices: 20 us -> 0 us
  between operations: 14.2 us -> 0.65 us
  matrix products: 9.32 us -> 0 us
  other arithmetic: 7.65 us -> 0 us
    all_to_all x2 -> x0, blocking collectives: 230 us -> none  [the longest x1 205 us: body(): lax.all_to_all(send_rows, 'expert', split_axis=0, concat_axis=1, tiled=True)]
    pallas_call x0 -> x1, Pallas kernels: none -> 110 us  [body(): pl.pallas_call(kernel, out_shape=(jax.ShapeDtypeStruct((NZ, CAP, SH), BF)...]
    psum x1 -> x0, blocking collectives: 23.8 us -> none  [gate_sum(): return lax.psum(gate_piece, 'dp')]
    all_to_all x1 -> x0, starting transfers between devices: 19.9 us -> none  [body(): lax.all_to_all(gate_total, 'expert', split_axis=1, concat_axis=0, tiled=T...]
    all_to_all x1 -> x0, waiting for transfers between devices: 18.8 us -> none  [body(): lax.all_to_all(gate_total, 'expert', split_axis=1, concat_axis=0, tiled=T...]
    gather x3 -> x0, local copies, waits for them, and re-layouts: 14.3 us -> none  [the longest x1 6.8 us: body(): gates.reshape(-1)[clipped]]
    unnamed x14 -> x13, local copies, waits for them, and re-layouts: 21.5 us -> 7.57 us
    dot_general x2 -> x0, matrix products: 9.32 us -> none  [the longest x1 5.62 us: body(): jnp.einsum('esf,esd->fed', hidden, scaled, preferred_element_type=jnp.flo...]
  transfers between devices with their start and end apart: 3 -> 0, of which waited for: 2 -> 0; matrix products, arithmetic and copies ran while one was open for 3% -> 0% of each run, Pallas kernels for 0% -> 0%
where the time goes in v1:
time: 118 us
  Pallas kernels  110 us (93%)
  local copies, waits for them, and re-layouts  7.57 us (6%)
    pallas_call x1, Pallas kernels, body(): pl.pallas_call(kernel, out_shape=(jax.ShapeDtypeStruct((NZ, CAP, SH), BF)...  110 us
    unnamed x13, local copies, waits for them, and re-layouts  7.57 us

profile of v1, /device:TPU:1, one launch (start us, length us, event | category | flops | bytes accessed | tf_op | source)
XLA Modules:
  0.0 118.0 jit_solution(14054214684245205954)
XLA Ops:
  0.6 0.0 copy-start
  0.6 1.6 %copy-done = bf16[1024,1024]{1,0:T(8,128)(2,1)S(1)} copy-done((bf16[1024,1024]{1,0:T(8,128)(2,1)S(1)}, bf16[1024,1024]{1,0:T(8,128)(2,1)}, u32[]{:S(2)}) %copy-start) | copy-done | bytes 2097176
  2.2 0.0 copy-start.1
  2.2 1.5 %copy-done.1 = bf16[1,1024,896]{2,1,0:T(8,128)(2,1)S(1)} copy-done((bf16[1,1024,896]{2,1,0:T(8,128)(2,1)S(1)}, bf16[1,1024,896]{2,1,0:T(8,128)(2,1)}, u32[]{:S(2)}) %copy-start.1) | copy-done | bytes 1835032
  3.7 0.0 copy-start.2
  3.7 0.9 copy-done.2
  4.6 0.0 copy-start.3
  4.6 0.7 copy-done.3
  5.3 0.0 copy-start.4
  5.3 0.7 copy-done.4
  6.0 109.7 %shard_map.76 = (bf16[32,32,128]{2,1,0:T(8,128)(2,1)S(1)}, f32[256,896]{1,0:T(8,128)S(1)}, f32[8,64]{1,0:T(8,128)S(1)}) custom-call(bf16[64,896]{1,0:T(8,128)(2,1)S(1)} %copy-done.2, s32[8,64]{1,0:T(8,128)S(1)} %bitcast.12, bf16[8,64]{1,0:T(8,128)(2,1)S(1)} %bitcast.13, bf16[32,32,1024]{2,1,0:T(8,128)(2,1)S(1)} %bitcast.10, bf16[4,2,128,896]{3,2,1,0:T(8,128)(2,1)S(1)} %bitcast.11), custom_call_target="tpu_custom_call" | custom-call | flops 3758096384 | bytes 6291456 | tf_op jit(solution)/shard_map/pallas_call | solution.py:417
  115.7 0.7 copy.11
  116.4 0.9 copy.12
  117.4 0.6 copy.13
Async XLA Ops:
  0.6 1.6 %copy-start = (bf16[1024,1024]{1,0:T(8,128)(2,1)S(1)}, bf16[1024,1024]{1,0:T(8,128)(2,1)}, u32[]{:S(2)}) copy-start(bf16[1024,1024]{1,0:T(8,128)(2,1)} %param.8) | copy-start | bytes 6291460
  2.2 1.5 %copy-start.1 = (bf16[1,1024,896]{2,1,0:T(8,128)(2,1)S(1)}, bf16[1,1024,896]{2,1,0:T(8,128)(2,1)}, u32[]{:S(2)}) copy-start(bf16[1,1024,896]{2,1,0:T(8,128)(2,1)} %param.9) | copy-start | bytes 5505028
  3.7 0.9 copy-start.2
  4.6 0.7 copy-start.3
  5.3 0.7 copy-start.4

commit v2 on v1

--- a/solution.py
+++ b/solution.py
@@ -32,9 +32,9 @@
 
 
 def kernel(
-    x_ref, ids_ref, gates_ref, hid_hbm, w_hbm,
+    x_hbm, ids_hbm, gates_hbm, hid_hbm, w_hbm,
     dh_ref, wg_ref, gg_ref,
-    gat, hid, wv, acc, rows_s, scaled_s, pown, sel_s, gcol_s,
+    gat, ids_ref, gates_ref, hid, wv, acc, rows_s, scaled_s, pown, sel_s, gcol_s, gsum,
     pbuf, prec, qbuf, qrec, gsend, gback, part_s, parts,
     xa, xb1, xb2, ra, rb1, rb2,
     load_sem, zs, zr, cs, cr, ys, yr, gs, gr, ps, pr, xs, xr,
@@ -51,6 +51,23 @@
     copp = lax.rem(cx + 2, NC)
     partner = dp + 1 - 2 * core
 
+    first = (
+        pltpu.make_async_copy(ids_hbm, ids_ref, load_sem.at[3]),
+        pltpu.make_async_copy(gates_hbm, gates_ref, load_sem.at[4]),
+    )
+    tiles = [
+        pltpu.make_async_copy(
+            x_hbm.at[:, pl.ds(j * 128, 128)],
+            gat.at[0, pl.ds(META + j * TOK, TOK)],
+            load_sem.at[5 + j],
+        )
+        for j in range(TILES)
+    ]
+    for load in first:
+        load.start()
+    for load in tiles:
+        load.start()
+
     barrier = pltpu.get_barrier_semaphore()
     for nb in (zright, zleft):
         pl.semaphore_signal(barrier, inc=1, device_id={"expert": nb}, device_id_type=MESH)
@@ -69,14 +86,17 @@
     for load in loads:
         load.start()
 
+    for load in first:
+        load.wait()
+
     e_iota = lax.broadcasted_iota(jnp.int32, (NZ, TOK), 0)
     gate_tab = jnp.zeros((NZ, TOK), F32)
     gates = gates_ref[...].astype(F32)
     for k in range(8):
         gate_tab = gate_tab + jnp.where(e_iota == ids_ref[k : k + 1, :], gates[k : k + 1, :], 0.0)
     gat[0, 0:META, :] = jnp.concatenate([gate_tab[0:META], gate_tab[META:]], axis=1).astype(BF)
-    for j in range(TILES):
-        gat[0, META + j * TOK : META + (j + 1) * TOK, :] = x_ref[:, j * 128 : (j + 1) * 128]
+    for load in tiles:
+        load.wait()
 
     pl.semaphore_wait(barrier, 4 + ND - 1)
 
@@ -103,8 +123,8 @@
         load.wait()
     acc[...] = jnp.zeros_like(acc)
 
-    def ring_step(k):
-        for c in range(NCH):
+    def ring_step(k, part):
+        for c in (0, 1) if part == 0 else (2, 3):
             hop(0, c, k).wait_recv()
 
             @pl.when(k < 15)
@@ -120,7 +140,7 @@
         dist = GB // 2 * g + (i + 1) // 2
         return lax.rem(z + dist if i % 2 == 0 else z - dist + NZ, NZ)
 
-    def rows_of_group(g):
+    def rows_of_group(g, h):
         base = g * GB
         lane = lax.broadcasted_iota(jnp.int32, (GB, 128), 1)
         row = lax.broadcasted_iota(jnp.int32, (GB, 128), 0)
@@ -139,32 +159,31 @@
         ).astype(jnp.int32)
         target = jnp.where(named, lax.rem(row, 4) * CAP + count, -1)
         slot = lax.broadcasted_iota(jnp.int32, (128, 128), 0)
-        for h in range(2):
-            sel, gsel = [], []
-            for j in range(2):
-                a = 4 * h + 2 * j
-                t = jnp.maximum(target[a : a + 1], target[a + 1 : a + 2])
-                gv = mine[a : a + 1] + mine[a + 1 : a + 2]
-                one = slot == t
-                sel.append(jnp.where(one, 1.0, 0.0))
-                gsel.append(jnp.where(one, gv, 0.0))
-            sel = jnp.concatenate(sel, axis=1)
-            gsel = jnp.concatenate(gsel, axis=1)
-            sel_s[h] = sel
-            gcol_s[h * 128 : (h + 1) * 128, :] = jnp.sum(gsel, axis=1, keepdims=True)
-            sel = sel.astype(BF)
-            gsel = gsel.astype(BF)
-            for j in range(TILES):
-                xt = gat[
-                    pl.ds(base + 4 * h, 4), META + j * TOK : META + (j + 1) * TOK, :
-                ].reshape(4 * TOK, 128)
-                cols = slice(j * 128, (j + 1) * 128)
-                rows_s[h * 128 : (h + 1) * 128, cols] = jnp.dot(
-                    sel, xt, preferred_element_type=F32
-                ).astype(BF)
-                scaled_s[h * 128 : (h + 1) * 128, cols] = jnp.dot(
-                    gsel, xt, preferred_element_type=F32
-                ).astype(BF)
+        sel, gsel = [], []
+        for j in range(2):
+            a = 4 * h + 2 * j
+            t = jnp.maximum(target[a : a + 1], target[a + 1 : a + 2])
+            gv = mine[a : a + 1] + mine[a + 1 : a + 2]
+            one = slot == t
+            sel.append(jnp.where(one, 1.0, 0.0))
+            gsel.append(jnp.where(one, gv, 0.0))
+        sel = jnp.concatenate(sel, axis=1)
+        gsel = jnp.concatenate(gsel, axis=1)
+        sel_s[h] = sel
+        gcol_s[h * 128 : (h + 1) * 128, :] = jnp.sum(gsel, axis=1, keepdims=True)
+        sel = sel.astype(BF)
+        gsel = gsel.astype(BF)
+        for j in range(TILES):
+            xt = gat[
+                pl.ds(base + 4 * h, 4), META + j * TOK : META + (j + 1) * TOK, :
+            ].reshape(4 * TOK, 128)
+            cols = slice(j * 128, (j + 1) * 128)
+            rows_s[h * 128 : (h + 1) * 128, cols] = jnp.dot(
+                sel, xt, preferred_element_type=F32
+            ).astype(BF)
+            scaled_s[h * 128 : (h + 1) * 128, cols] = jnp.dot(
+                gsel, xt, preferred_element_type=F32
+            ).astype(BF)
 
     def partial_of(which, y):
         return lax.dot_general(
@@ -191,14 +210,45 @@
             device_id_type=MESH,
         )
 
+    def hidden_cols(g, unit):
+        cols = pl.ds(pl.multiple_of(unit * SH, SH), SH)
+        return jnp.concatenate(
+            [hid[source_of(g, i), :, cols] for i in range(GB)], axis=0
+        ).astype(F32)
+
     def send_partials(g):
+        mine = jnp.zeros((GR, SH), F32)
         for y in range(4):
-            pbuf[g, y] = partial_of(1, y).astype(BF)
+            part = partial_of(1, y).astype(BF)
+            pbuf[g, y] = part
+            mine = mine + hidden_cols(g, 2 * y + 1 - core) * part.astype(F32)
+        gsum[...] = mine
         to_partner(g).start()
 
-    def own_partials():
+    def own_partials(g):
+        mine = gsum[...]
         for y in range(4):
-            pown[y] = partial_of(0, y).astype(BF)
+            part = partial_of(0, y).astype(BF)
+            pown[y] = part
+            mine = mine + hidden_cols(g, 2 * y + core) * part.astype(F32)
+        col = jnp.sum(mine, axis=1, keepdims=True)
+        for h in range(2):
+            back = jnp.sum(sel_s[h] * col[h * 128 : (h + 1) * 128], axis=0, keepdims=True)
+            for j in range(2):
+                gsend[g * 4 + 2 * h + j] = back[:, j * 128 : (j + 1) * 128]
+        for i in range(GB):
+            p = g * GB + i
+            if i == 0:
+
+                @pl.when(g > 0)
+                def _():
+                    to_home(p, source_of(g, i)).start()
+
+                @pl.when(g == 0)
+                def _():
+                    gback[z] = gsend[0]
+            else:
+                to_home(p, source_of(g, i)).start()
 
     def contribute(g, share):
         parts_h = [
@@ -234,61 +284,28 @@
             to_y(g, i).wait_recv()
             total = total + qrec[g, i - 1].astype(F32)
         dh = (gcol_s[...] * total).astype(BF)
-        own = []
         for i in range(GB):
-            s = source_of(g, i)
-            dh_ref[s] = dh[i * CAP : (i + 1) * CAP]
-            own.append(hid[s, :, pl.ds(pl.multiple_of(dp * SH, SH), SH)])
-        own = jnp.concatenate(own, axis=0).astype(F32)
-        col = jnp.sum(own * total, axis=1, keepdims=True)
-        for h in range(2):
-            back = jnp.sum(sel_s[h] * col[h * 128 : (h + 1) * 128], axis=0, keepdims=True)
-            for j in range(2):
-                gsend[g * 4 + 2 * h + j] = back[:, j * 128 : (j + 1) * 128]
-        for i in range(GB):
-            p = g * GB + i
-            if i == 0:
-
-                @pl.when(g > 0)
-                def _():
-                    to_home(p, source_of(g, i)).start()
-
-                @pl.when(g == 0)
-                def _():
-                    gback[z] = gsend[0]
-            else:
-                to_home(p, source_of(g, i)).start()
+            dh_ref[source_of(g, i)] = dh[i * CAP : (i + 1) * CAP]
+
+    pieces = (
+        lambda g: rows_of_group(g, 0),
+        lambda g: rows_of_group(g, 1),
+        send_partials,
+        own_partials,
+        lambda g: (sum_cores(g), contribute(g, jnp.int32(0))),
+        lambda g: contribute(g, jnp.int32(1)),
+        lambda g: contribute(g, jnp.int32(2)),
+        lambda g: (contribute(g, jnp.int32(3)), finish_rows(g)),
+    )
 
     @pl.loop(0, NG)
     def _(g):
-        ring_step(4 * g)
-
-        @pl.when(g > 0)
-        def _():
-            rows_of_group(g - 1)
-            send_partials(g - 1)
-
-        ring_step(4 * g + 1)
-
-        @pl.when(g > 0)
-        def _():
-            own_partials()
-            contribute(g - 1, jnp.int32(0))
-            contribute(g - 1, jnp.int32(1))
-
-        ring_step(4 * g + 2)
-
-        @pl.when(g > 0)
-        def _():
-            contribute(g - 1, jnp.int32(2))
-            contribute(g - 1, jnp.int32(3))
-            sum_cores(g - 1)
-
-        ring_step(4 * g + 3)
-
-        @pl.when(g > 0)
-        def _():
-            finish_rows(g - 1)
+        for i, piece in enumerate(pieces):
+            ring_step(4 * g + i // 2, i % 2)
+
+            @pl.when(g > 0)
+            def _():
+                piece(g - 1)
 
     half = FQ // 2
 
@@ -305,27 +322,28 @@
         )
 
     last = jnp.int32(NG - 1)
-    rows_of_group(last)
+    rows_of_group(last, 0)
+    rows_of_group(last, 1)
     contribute(last, copp)
     for d in range(2):
         xa[d] = acc[copp, d * half : (d + 1) * half].astype(BF)
         to_x(0, d).start()
     send_partials(last)
+    own_partials(last)
     contribute(last, cright)
     contribute(last, cleft)
     xb1[0] = acc[cright, half:].astype(BF)
     to_x(1, 0).start()
     xb1[1] = acc[cleft, :half].astype(BF)
     to_x(1, 1).start()
-    own_partials()
     sum_cores(last)
+    contribute(last, cx)
     to_x(0, 0).wait_recv()
     xb2[0] = (acc[cright, :half] + ra[0].astype(F32)).astype(BF)
     to_x(2, 0).start()
     to_x(0, 1).wait_recv()
     xb2[1] = (acc[cleft, half:] + ra[1].astype(F32)).astype(BF)
     to_x(2, 1).start()
-    contribute(last, cx)
     finish_rows(last)
 
     def from_home(e):
@@ -421,10 +439,12 @@
             jax.ShapeDtypeStruct((FQ, WID), F32),
             jax.ShapeDtypeStruct((8, TOK), F32),
         ),
-        in_specs=[vmem, vmem, vmem, any_spec, any_spec],
+        in_specs=[any_spec] * 5,
         out_specs=[vmem, vmem, vmem],
         scratch_shapes=[
             pltpu.VMEM((NZ, ROWS, 128), BF),
+            pltpu.VMEM((8, TOK), jnp.int32),
+            pltpu.VMEM((8, TOK), BF),
             pltpu.VMEM((NZ, CAP, FF), BF),
             pltpu.VMEM((2, 4, SH, WID), BF),
             pltpu.VMEM((NC, FQ, WID), F32),
@@ -433,6 +453,7 @@
             pltpu.VMEM((4, GR, SH), BF),
             pltpu.VMEM((2, 128, 256), F32),
             pltpu.VMEM((GR, 1), F32),
+            pltpu.VMEM((GR, SH), F32),
             pltpu.VMEM((NG, 4, GR, SH), BF),
             pltpu.VMEM((NG, 4, GR, SH), BF),
             pltpu.VMEM((NG, 3, GR, SH), BF),
@@ -447,7 +468,7 @@
             pltpu.VMEM((2, half, WID), BF),
             pltpu.VMEM((2, half, WID), BF),
             pltpu.VMEM((2, half, WID), BF),
-            dma((3,)),
+            dma((5 + TILES,)),
             dma((2, NCH, 16)),
             dma((2, NCH, 16)),
             dma((NG,)),
@@ -462,7 +483,7 @@
             dma((3, 2)),
         ],
         compiler_params=pltpu.CompilerParams(
-            collective_id=0, has_side_effects=True, vmem_limit_bytes=48 * 2**20
+            collective_id=0, has_side_effects=True, vmem_limit_bytes=60 * 2**20
         ),
         cost_estimate=pl.CostEstimate(
             flops=4 * 1024 * 1024 * 896, bytes_accessed=6 * 2**20, transcendentals=0

time: 118 us -> 108 us (0.915)
  Pallas kernels: 110 us -> 103 us
  local copies, waits for them, and re-layouts: 7.57 us -> 4.43 us
    pallas_call x1, Pallas kernels: 110 us -> 103 us  [body(): pl.pallas_call(kernel, out_shape=(jax.ShapeDtypeStruct((NZ, CAP, SH), BF)...]
    unnamed x13 -> x5, local copies, waits for them, and re-layouts: 7.57 us -> 4.43 us
where the time goes in v2:
time: 108 us
  Pallas kernels  103 us (95%)
  local copies, waits for them, and re-layouts  4.43 us (4%)
    pallas_call x1, Pallas kernels, body(): pl.pallas_call(kernel, out_shape=(jax.ShapeDtypeStruct((NZ, CAP, SH), BF)...  103 us
    unnamed x5, local copies, waits for them, and re-layouts  4.43 us

profile of v2, /device:TPU:1, one launch (start us, length us, event | category | flops | bytes accessed | tf_op | source)
XLA Modules:
  0.0 107.9 jit_solution(605399753764521246)
XLA Ops:
  0.6 102.8 %shard_map.76 = (bf16[32,32,128]{2,1,0:T(8,128)(2,1)}, f32[256,896]{1,0:T(8,128)}, f32[8,64]{1,0:T(8,128)}) custom-call(bf16[64,896]{1,0:T(8,128)(2,1)} %x_hbm.1, s32[8,64]{1,0:T(8,128)} %bitcast.12, bf16[8,64]{1,0:T(8,128)(2,1)} %bitcast.13, bf16[32,32,1024]{2,1,0:T(8,128)(2,1)} %bitcast.10, bf16[4,2,128,896]{3,2,1,0:T(8,128)(2,1)} %bitcast.11), custom_call_target="tpu_custom_call" | custom-call | flops 3758096384 | bytes 6291456 | tf_op jit(solution)/shard_map/pallas_call | solution.py:435
  103.5 0.0 copy-start
  103.5 1.7 %copy.11 = bf16[1024,128]{1,0:T(8,128)(2,1)} copy(bf16[1024,128]{1,0:T(8,128)(2,1)} %bitcast.8) | data formatting | bytes 524288
  105.1 2.2 %copy.12 = f32[1,256,896]{2,1,0:T(8,128)} copy(f32[1,256,896]{2,1,0:T(8,128)} %bitcast.7) | data formatting | bytes 1835008
  107.3 0.0 copy-done
  107.3 0.6 copy.13
Async XLA Ops:
  103.5 3.8 %copy-start = (f32[8,64]{1,0:T(8,128)S(1)}, f32[8,64]{1,0:T(8,128)}, u32[]{:S(2)}) copy-start(f32[8,64]{1,0:T(8,128)} %get-tuple-element.8) | copy-start | bytes 6148

commit v3 on v2

--- a/solution.py
+++ b/solution.py
@@ -27,7 +27,7 @@
 NG = NZ // GB
 GR = GB * CAP
 GT = GB * TOK
-CHUNKS = ((0, META + 2 * TOK), (META + 2 * TOK, 2 * TOK), (META + 4 * TOK, 2 * TOK), (META + 6 * TOK, TOK))
+CHUNKS = ((0, META + TOK), (META + TOK, 2 * TOK), (META + 3 * TOK, 2 * TOK), (META + 5 * TOK, 2 * TOK))
 NCH = len(CHUNKS)
 
 
@@ -105,7 +105,7 @@
         if d == 0:
             src, dst, dev = jnp.maximum(2 * k - 1, 0), 2 * k + 1, zright
         else:
-            src, dst, dev = 2 * k, 2 * k + 2, zleft
+            src, dst, dev = 2 * k, jnp.minimum(2 * k + 2, NZ - 1), zleft
         return pltpu.make_async_remote_copy(
             src_ref=gat.at[src, pl.ds(lo, n)],
             dst_ref=gat.at[dst, pl.ds(lo, n)],
@@ -125,16 +125,16 @@
 
     def ring_step(k, part):
         for c in (0, 1) if part == 0 else (2, 3):
-            hop(0, c, k).wait_recv()
-
-            @pl.when(k < 15)
-            def _():
-                hop(0, c, k + 1).start()
-                hop(1, c, k).wait_recv()
-
-            @pl.when(k < 14)
-            def _():
-                hop(1, c, k + 1).start()
+            for d in range(2):
+                hops = 16 if c // 2 == d else 15
+
+                @pl.when(k < hops)
+                def _():
+                    hop(d, c, k).wait_recv()
+
+                @pl.when(k < hops - 1)
+                def _():
+                    hop(d, c, k + 1).start()
 
     def source_of(g, i):
         dist = GB // 2 * g + (i + 1) // 2
@@ -404,11 +404,12 @@
     @pl.loop(0, 16)
     def _(k):
         for c in range(NCH):
-            hop(0, c, k).wait_send()
-
-            @pl.when(k < 15)
-            def _():
-                hop(1, c, k).wait_send()
+            for d in range(2):
+                hops = 16 if c // 2 == d else 15
+
+                @pl.when(k < hops)
+                def _():
+                    hop(d, c, k).wait_send()
 
     @pl.loop(0, NG)
     def _(g):
@@ -435,9 +436,9 @@
     d_hidden, w_grad, gate_grad = pl.pallas_call(
         kernel,
         out_shape=(
-            jax.ShapeDtypeStruct((NZ, CAP, SH), BF),
-            jax.ShapeDtypeStruct((FQ, WID), F32),
-            jax.ShapeDtypeStruct((8, TOK), F32),
+            pltpu.VMEM((NZ, CAP, SH), BF),
+            pltpu.VMEM((FQ, WID), F32),
+            pltpu.VMEM((8, TOK), F32),
         ),
         in_specs=[any_spec] * 5,
         out_specs=[vmem, vmem, vmem],

time: 108 us -> 104 us (0.963)
  local copies, waits for them, and re-layouts: 4.43 us -> 2.22 us
  Pallas kernels: 103 us -> 101 us
    unnamed x5 -> x3, local copies, waits for them, and re-layouts: 4.43 us -> 2.22 us
    pallas_call x1, Pallas kernels: 103 us -> 101 us  [body(): pl.pallas_call(kernel, out_shape=(pltpu.VMEM((NZ, CAP, SH), BF), pltpu.VM...]
where the time goes in v3:
time: 104 us; the launch traced here: 103 us
  Pallas kernels  101 us (97%)
  local copies, waits for them, and re-layouts  2.22 us (2%)
    pallas_call x1, Pallas kernels, body(): pl.pallas_call(kernel, out_shape=(pltpu.VMEM((NZ, CAP, SH), BF), pltpu.VM...  101 us
    unnamed x3, local copies, waits for them, and re-layouts  2.22 us

profile of v3, /device:TPU:1, one launch (start us, length us, event | category | flops | bytes accessed | tf_op | source)
XLA Modules:
  0.0 103.5 jit_solution(15415790543510684894)
XLA Ops:
  0.6 100.6 %shard_map.76 = (bf16[32,32,128]{2,1,0:T(8,128)(2,1)S(1)}, f32[256,896]{1,0:T(8,128)S(1)}, f32[8,64]{1,0:T(8,128)S(1)}) custom-call(bf16[64,896]{1,0:T(8,128)(2,1)} %x_hbm.1, s32[8,64]{1,0:T(8,128)} %bitcast.12, bf16[8,64]{1,0:T(8,128)(2,1)} %bitcast.13, bf16[32,32,1024]{2,1,0:T(8,128)(2,1)} %bitcast.10, bf16[4,2,128,896]{3,2,1,0:T(8,128)(2,1)} %bitcast.11), custom_call_target="tpu_custom_call" | custom-call | flops 3758096384 | bytes 6291456 | tf_op jit(solution)/shard_map/pallas_call | solution.py:436
  101.3 0.7 copy.11
  102.0 0.9 copy.12
  102.9 0.6 copy.13

commit v4 on v3

--- a/solution.py
+++ b/solution.py
@@ -144,9 +144,10 @@
         base = g * GB
         lane = lax.broadcasted_iota(jnp.int32, (GB, 128), 1)
         row = lax.broadcasted_iota(jnp.int32, (GB, 128), 0)
-        tab = gat[pl.ds(base, GB), 0:META, :].astype(F32)
-        sub = lax.broadcasted_iota(jnp.int32, (GB, META, 128), 1)
+        tab = gat[pl.ds(base + 4 * h, 4), 0:META, :].astype(F32)
+        sub = lax.broadcasted_iota(jnp.int32, (4, META, 128), 1)
         mine = jnp.sum(jnp.where(sub == lax.rem(z, META), tab, 0.0), axis=1)
+        mine = jnp.concatenate([mine, mine], axis=0)
         odd = lax.rem(row, 2)
         mine = jnp.where(odd == z // META, mine, pltpu.roll(mine, TOK, 1))
         mine = jnp.where(lane // TOK == odd, mine, 0.0)
@@ -161,7 +162,7 @@
         slot = lax.broadcasted_iota(jnp.int32, (128, 128), 0)
         sel, gsel = [], []
         for j in range(2):
-            a = 4 * h + 2 * j
+            a = 2 * j
             t = jnp.maximum(target[a : a + 1], target[a + 1 : a + 2])
             gv = mine[a : a + 1] + mine[a + 1 : a + 2]
             one = slot == t
@@ -301,7 +302,13 @@
     @pl.loop(0, NG)
     def _(g):
         for i, piece in enumerate(pieces):
-            ring_step(4 * g + i // 2, i % 2)
+            if i < 6:
+                ring_step(4 * g + i // 2, i % 2)
+            else:
+
+                @pl.when(g < NG - 1)
+                def _():
+                    ring_step(4 * g + 3, i % 2)
 
             @pl.when(g > 0)
             def _():
@@ -323,6 +330,8 @@
 
     last = jnp.int32(NG - 1)
     rows_of_group(last, 0)
+    for part in range(2):
+        ring_step(jnp.int32(15), part)
     rows_of_group(last, 1)
     contribute(last, copp)
     for d in range(2):
@@ -344,6 +353,17 @@
     to_x(0, 1).wait_recv()
     xb2[1] = (acc[cleft, half:] + ra[1].astype(F32)).astype(BF)
     to_x(2, 1).start()
+
+    @pl.loop(0, 16)
+    def _(k):
+        for c in range(NCH):
+            for d in range(2):
+                hops = 16 if c // 2 == d else 15
+
+                @pl.when(k < hops)
+                def _():
+                    hop(d, c, k).wait_send()
+
     finish_rows(last)
 
     def from_home(e):
@@ -386,6 +406,16 @@
     for i in range(1, ND):
         to_dp(i).start()
 
+    @pl.loop(0, NG)
+    def _(g):
+        to_partner(g).wait_send()
+        for i in range(1, 4):
+            to_y(g, i).wait_send()
+
+    @pl.loop(1, NZ)
+    def _(p):
+        to_home(p, zright).wait_send()
+
     to_x(1, 0).wait_recv()
     to_x(1, 1).wait_recv()
     to_x(2, 0).wait_recv()
@@ -400,26 +430,6 @@
         i = lax.rem(dp - j + ND, ND)
         total = total + jnp.where(i == 0, part_s[...], parts[jnp.maximum(i - 1, 0)])
     gg_ref[...] = total[:, 0:TOK]
-
-    @pl.loop(0, 16)
-    def _(k):
-        for c in range(NCH):
-            for d in range(2):
-                hops = 16 if c // 2 == d else 15
-
-                @pl.when(k < hops)
-                def _():
-                    hop(d, c, k).wait_send()
-
-    @pl.loop(0, NG)
-    def _(g):
-        to_partner(g).wait_send()
-        for i in range(1, 4):
-            to_y(g, i).wait_send()
-
-    @pl.loop(1, NZ)
-    def _(p):
-        to_home(p, zright).wait_send()
 
     for i in range(1, ND):
         to_dp(i).wait_send()

time: 104 us -> 103 us (level)
  Pallas kernels: 101 us -> 99.9 us
where the time goes in v4:
time: 103 us
  Pallas kernels  99.9 us (97%)
  local copies, waits for them, and re-layouts  2.22 us (2%)
    pallas_call x1, Pallas kernels, body(): pl.pallas_call(kernel, out_shape=(pltpu.VMEM((NZ, CAP, SH), BF), pltpu.VM...  99.9 us
    unnamed x3, local copies, waits for them, and re-layouts  2.22 us

profile of v4, /device:TPU:1, one launch (start us, length us, event | category | flops | bytes accessed | tf_op | source)
XLA Modules:
  0.0 102.8 jit_solution(8258421973017420515)
XLA Ops:
  0.6 99.9 %shard_map.76 = (bf16[32,32,128]{2,1,0:T(8,128)(2,1)S(1)}, f32[256,896]{1,0:T(8,128)S(1)}, f32[8,64]{1,0:T(8,128)S(1)}) custom-call(bf16[64,896]{1,0:T(8,128)(2,1)} %x_hbm.1, s32[8,64]{1,0:T(8,128)} %bitcast.12, bf16[8,64]{1,0:T(8,128)(2,1)} %bitcast.13, bf16[32,32,1024]{2,1,0:T(8,128)(2,1)} %bitcast.10, bf16[4,2,128,896]{3,2,1,0:T(8,128)(2,1)} %bitcast.11), custom_call_target="tpu_custom_call" | custom-call | flops 3758096384 | bytes 6291456 | tf_op jit(solution)/shard_map/pallas_call | solution.py:446
  100.5 0.7 copy.11
  101.3 0.9 copy.12
  102.2 0.6 copy.13
